TPU v7x, 32 devices: a whole 2x2x4 slice. The times are simulated.
32 devices in a mesh: outer: 8 (over y, x, core), inner: 4 (over z).
Axes of the slice: x: 2, y: 2, z: 4, core: 2. Of those that a mesh axis runs over, the one named last changes fastest.
Arguments:
- gate: float32 [128, 16384], P(None, ('outer', 'inner')), may hold values from -6 to 6
- keys: float32 [128, 16384], P(None, ('outer', 'inner')), may hold values from -6 to 6
- values: float32 [128, 16384], P(None, ('outer', 'inner')), may hold values from -6 to 6
- taps: float32 [128, 16384], P(None, ('outer', 'inner')), may hold values from -0.046875 to 0.046875
- skip_gain: float32 [128], replicated, may hold values from 0.5 to 2
Outputs:
- mixed: float32 [128, 16384], P(None, ('outer', 'inner'))
All inputs are finite; a program needn't handle non-finite values.
Results may differ from a plain program's by a relative error of at most 0.000053.
Values sent between devices are 32-bit elements; how exact they have to be, the bound alone decides.
No kernel may reach another device: no remote copies, remote signals or barrier semaphores. Data moves between devices by JAX's collectives and lax.ppermute only.
A program may use at most 64 MiB of HBM per device.

v0:
```python
from functools import partial
import math

import jax
import jax.numpy as jnp
import ml_dtypes
import numpy as np
from jax import lax
from jax.experimental import pallas as pl
from jax.experimental.pallas import tpu as pltpu
from jax.sharding import PartitionSpec as P

LANES = 128
AXES = ("outer", "inner")

TWO_PI = 2.0 * math.pi
HIGHEST = lax.Precision.HIGHEST


def table(count_a, count_b, modulus, sign):
    left = lax.broadcasted_iota(jnp.int32, (count_a, count_b), 0)
    right = lax.broadcasted_iota(jnp.int32, (count_a, count_b), 1)
    phase = TWO_PI / modulus * (left * right % modulus).astype(jnp.float32)
    return (jnp.cos(phase), sign * jnp.sin(phase))


def mix(form, cosine, sine, real, imag):
    contract = partial(jnp.einsum, precision=HIGHEST)
    return (
        contract(form, cosine, real) - contract(form, sine, imag),
        contract(form, sine, real) + contract(form, cosine, imag),
    )


def rotate(real, imag, cosine, sine):
    return (real * cosine - imag * sine, real * sine + imag * cosine)


def forward_rows(real, imag):
    split = 16
    lead = real.shape[:-1]
    size = real.shape[-1]
    short = size // split
    real = real.reshape(lead + (split, short))
    imag = imag.reshape(lead + (split, short))
    cosine, sine = table(split, split, split, -1.0)
    real, imag = mix("ka,...as->...ks", cosine, sine, real, imag)
    cosine, sine = table(split, short, size, -1.0)
    real, imag = rotate(real, imag, cosine, sine)
    cosine, sine = table(short, short, short, -1.0)
    real, imag = mix("sb,...ks->...bk", cosine, sine, real, imag)
    return (real.reshape(lead + (size,)), imag.reshape(lead + (size,)))


def inverse_rows(real, imag):
    split = 16
    lead = real.shape[:-1]
    size = real.shape[-1]
    short = size // split
    real = real.reshape(lead + (short, split))
    imag = imag.reshape(lead + (short, split))
    cosine, sine = table(short, short, short, 1.0)
    real, imag = mix("sb,...bk->...sk", cosine, sine, real, imag)
    cosine, sine = table(short, split, size, 1.0)
    real, imag = rotate(real, imag, cosine, sine)
    cosine, sine = table(split, split, split, 1.0)
    real, imag = mix("ak,...sk->...as", cosine, sine, real, imag)
    return (real.reshape(lead + (size,)), imag.reshape(lead + (size,)))


def by_sections(gate, keys, values, taps, skip_gain):
    inner_count = lax.axis_size("inner")
    devices = lax.axis_size("outer") * inner_count
    rank = lax.axis_index("outer") * inner_count + lax.axis_index("inner")
    chans, seg = keys.shape
    both = 2 * chans
    cols = seg // devices
    blocks = 2 * devices
    full = blocks * seg
    contract = partial(jnp.einsum, precision=HIGHEST)
    product = keys * values
    source = jnp.concatenate([product, taps], axis=0)
    sectioned = lax.all_to_all(
        lax.all_to_all(
            source.reshape(both, 1, 1, seg), "outer", split_axis=3, concat_axis=1, tiled=True
        ),
        "inner",
        split_axis=3,
        concat_axis=2,
        tiled=True,
    )
    sectioned = sectioned.reshape(both, devices, cols)
    cosine, sine = table(blocks, devices, blocks, -1.0)
    real = contract("km,cmj->ckj", cosine, sectioned)
    imag = contract("km,cmj->ckj", sine, sectioned)
    offset = rank * cols + lax.broadcasted_iota(jnp.int32, (blocks, cols), 1)
    residue = lax.broadcasted_iota(jnp.int32, (blocks, cols), 0)
    phase = TWO_PI / full * (offset * residue).astype(jnp.float32)
    real, imag = rotate(real, imag, jnp.cos(phase)[None], -jnp.sin(phase)[None])
    outgoing = jnp.stack([real, imag]).reshape(2, both, blocks, 1, 1, cols)
    moved = lax.all_to_all(
        lax.all_to_all(outgoing, "outer", split_axis=2, concat_axis=3, tiled=True),
        "inner",
        split_axis=2,
        concat_axis=4,
        tiled=True,
    )
    moved = moved.reshape(2, both, 2, seg)
    spec_real, spec_imag = forward_rows(moved[0], moved[1])
    sig_real, filt_real = (spec_real[:chans], spec_real[chans:])
    sig_imag, filt_imag = (spec_imag[:chans], spec_imag[chans:])
    real = sig_real * filt_real - sig_imag * filt_imag
    imag = sig_real * filt_imag + sig_imag * filt_real
    real, imag = inverse_rows(real, imag)
    residue = 2 * rank + lax.broadcasted_iota(jnp.int32, (2, seg), 0)
    offset = lax.broadcasted_iota(jnp.int32, (2, seg), 1)
    phase = TWO_PI / full * (offset * residue).astype(jnp.float32)
    real, imag = rotate(real, imag, jnp.cos(phase)[None], jnp.sin(phase)[None])
    returning = jnp.stack([real, imag]).reshape(2, chans, 1, 1, 2, seg)
    gathered = lax.all_to_all(
        lax.all_to_all(returning, "outer", split_axis=5, concat_axis=2, tiled=True),
        "inner",
        split_axis=5,
        concat_axis=3,
        tiled=True,
    )
    gathered = gathered.reshape(2, chans, blocks, cols)
    cosine, sine = table(devices, blocks, blocks, 1.0)
    conv = contract("mk,ckj->cmj", cosine, gathered[0]) - contract("mk,ckj->cmj", sine, gathered[1])
    conv = conv * (1.0 / full)
    conv = lax.all_to_all(
        lax.all_to_all(
            conv.reshape(chans, devices, 1, 1, cols),
            "outer",
            split_axis=1,
            concat_axis=2,
            tiled=True,
        ),
        "inner",
        split_axis=1,
        concat_axis=3,
        tiled=True,
    )
    conv = conv.reshape(chans, seg)
    return gate * (conv + skip_gain[:, None] * product)


def halves(array):
    high = array.astype(ml_dtypes.bfloat16)
    low = (array - high.astype(np.float64)).astype(ml_dtypes.bfloat16)
    return high, low


def transform_tables(devices, seg):
    length = devices * seg
    count = length // LANES
    odd = 2 * np.arange(count) + 1
    angle = 2 * np.pi / (4 * count) * ((odd[:, None] * np.arange(count)[None, :]) % (4 * count))
    first = np.concatenate([np.cos(angle), -np.sin(angle)], axis=0)
    last = np.concatenate([np.cos(angle).T, -np.sin(angle).T], axis=1) / length
    angle = 2 * np.pi / (4 * length) * ((odd[:, None] * np.arange(LANES)[None, :]) % (4 * length))
    twiddle = np.stack([np.cos(angle), np.sin(angle)]).astype(np.float32)
    angle = 2 * np.pi / LANES * ((np.arange(LANES)[:, None] * np.arange(LANES)[None, :]) % LANES)
    cosine, sine = np.cos(angle), np.sin(angle)
    rows = np.block([[cosine, -sine], [sine, cosine]])
    back = np.block([[cosine, sine], [-sine, cosine]])
    first_high, first_low = halves(first)
    rows_high, rows_low = halves(rows)
    back_high, back_low = halves(back)
    last_high, last_low = halves(last)
    return (
        np.concatenate([first_high, first_high, first_low, first_low], axis=1),
        np.concatenate([rows_high, rows_high, rows_high, rows_low], axis=0),
        np.concatenate([back_high, back_high, back_low], axis=0),
        np.concatenate([last_high, last_high, last_low], axis=1),
        twiddle,
    )


def send_orders(outer, inner):
    half = inner // 2
    turns = [at // 2 + half * (at % 2) for at in range(2 * half)] + list(range(2 * half, inner))
    ring = [at ^ (at >> 1) for at in range(outer)] if outer & (outer - 1) == 0 else list(range(outer))
    first = [at * inner + step for at in ring[:1] + ring[:0:-1] for step in range(inner)]
    second = [at * inner + step for at in range(outer) for step in turns[1:] + turns[:1]]
    return first, second


def split(array, count=2):
    parts = []
    for _ in range(count):
        parts.append(array.astype(jnp.bfloat16))
        array = array - parts[-1].astype(jnp.float32)
    return parts


def dot(left, right):
    return jnp.dot(left, right, preferred_element_type=jnp.float32)


def convolve_kernel(
    devices, chans, seg, data_ref, first_ref, rows_ref, back_ref, last_ref, twiddle_ref, out_ref, signal_ref
):
    parts = seg // LANES
    count = devices * parts
    cosine, sine = twiddle_ref[0], twiddle_ref[1]

    def lanes(at):
        return slice(at * LANES, (at + 1) * LANES)

    first, second = send_orders(lax.axis_size("outer"), lax.axis_size("inner"))

    groups = chans
    each = chans // groups
    at = range(groups)
    for group in at:
        for kind in range(2):
            for chan in range(each):
                for device in range(devices):
                    came = ((device * 2 + kind) * chans + group * each + chan) * parts
                    to = first[device] * parts
                    signal_ref[group, to : to + parts, lanes(kind * each + chan)] = data_ref[came : came + parts, :]

    def start(group):
        high, low = split(signal_ref[group])
        return dot(first_ref[...], jnp.concatenate([high, low, high, low], axis=0))

    def spectra(begun):
        turned = []
        for signal in range(2 * each):
            real, imag = begun[:count, lanes(signal)], begun[count:, lanes(signal)]
            turned.append(jnp.concatenate([real * cosine + imag * sine, imag * cosine - real * sine], axis=1))
        high, low, rest = split(jnp.concatenate(turned, axis=0), 3)
        return dot(jnp.concatenate([high, low, rest, high], axis=1), rows_ref[...])

    def back(spectrum):
        mid = each * count
        sig_real, sig_imag = spectrum[:mid, :LANES], spectrum[:mid, LANES:]
        filt_real, filt_imag = spectrum[mid:, :LANES], spectrum[mid:, LANES:]
        real = sig_real * filt_real - sig_imag * filt_imag
        imag = sig_real * filt_imag + sig_imag * filt_real
        high, low = split(jnp.concatenate([real, imag], axis=1))
        return dot(jnp.concatenate([high, low, high], axis=1), back_ref[...])

    def end(backed):
        turned = []
        for chan in range(each):
            real = backed[chan * count : (chan + 1) * count, :LANES]
            imag = backed[chan * count : (chan + 1) * count, LANES:]
            turned.append(jnp.concatenate([real * cosine - imag * sine, imag * cosine + real * sine], axis=0))
        high, low = split(jnp.concatenate(turned, axis=1))
        return dot(last_ref[...], jnp.concatenate([high, low, high], axis=0))

    begun = [start(group) for group in at]
    spectrum = [spectra(begun[group]) for group in at]
    backed = [back(spectrum[group]) for group in at]
    conv = [end(backed[group]) for group in at]
    for group in at:
        for chan in range(each):
            own = group * each + chan
            for device in range(devices):
                to = (device * chans + own) * parts
                came = second[device] * parts
                out_ref[to : to + parts, :] = conv[group][came : came + parts, lanes(chan)]


def gather_kernel(order, product_ref, taps_ref, out_ref):
    rows = product_ref.shape[0] * product_ref.shape[1] // LANES // len(order)
    for kind, ref in enumerate((product_ref, taps_ref)):
        source = ref[...].reshape(len(order) * rows, LANES)
        for at, rank in enumerate(order):
            to = (2 * at + kind) * rows
            out_ref[to : to + rows, :] = source[rank * rows : (rank + 1) * rows]


def gate_kernel(order, gate_ref, skip_ref, conv_ref, out_hbm, out_ref, sems):
    chans, seg = gate_ref.shape
    pieces = sems.shape[0]
    step = chans // pieces
    rows = conv_ref.shape[0] // len(order)
    each = len(order) // pieces
    place = {rank: at * rows for at, rank in enumerate(order)}
    copies = []
    for piece in range(pieces):
        at = slice(piece * step, (piece + 1) * step)
        came = [conv_ref[place[rank] : place[rank] + rows, :] for rank in range(piece * each, (piece + 1) * each)]
        conv = jnp.concatenate(came, axis=0).reshape(step, seg)
        out_ref[at, :] = gate_ref[at, :] * (conv + skip_ref[at, :])
        copies.append(pltpu.make_async_copy(out_ref.at[at, :], out_hbm.at[at, :], sems.at[piece]))
        copies[piece].start()
    for copy in copies:
        copy.wait()


def on_core(kernel, shape, moved, flops=10**6, scratch=(), **more):
    return pl.pallas_call(
        kernel,
        out_shape=jax.ShapeDtypeStruct(shape, jnp.float32),
        scratch_shapes=scratch,
        compiler_params=pltpu.CompilerParams(vmem_limit_bytes=32 * 2**20),
        cost_estimate=pl.CostEstimate(flops=flops, bytes_accessed=moved, transcendentals=0),
        **more,
    )


def by_channels(gate, keys, values, taps, skip_gain):
    devices = lax.axis_size("outer") * lax.axis_size("inner")
    chans, seg = keys.shape
    own = chans // devices
    tiles = seg // LANES
    tables = [jnp.asarray(table) for table in transform_tables(devices, seg)]
    orders = send_orders(lax.axis_size("outer"), lax.axis_size("inner"))

    def regroup(rows, order):
        return lax.all_to_all(rows, AXES, split_axis=0, concat_axis=0, tiled=True, axis_index_groups=[order])

    product = keys * values
    product, skip = lax.optimization_barrier((product, skip_gain[:, None] * product))
    sent = on_core(partial(gather_kernel, orders[0]), (2 * chans * tiles, LANES), 4 * chans * seg * 4)(product, taps)
    groups = own
    conv = on_core(
        partial(convolve_kernel, devices, own, seg),
        (chans * tiles, LANES),
        2 * 10**6,
        10**9,
        [pltpu.VMEM((groups, devices * tiles, 2 * own // groups * LANES), jnp.float32)],
    )(regroup(sent, orders[0]), *tables)
    pieces = 4
    return on_core(
        partial(gate_kernel, orders[1]),
        (chans, seg),
        4 * chans * seg * 4,
        scratch=[pltpu.VMEM((chans, seg), jnp.float32), pltpu.SemaphoreType.DMA((pieces,))],
        out_specs=pl.BlockSpec(memory_space=pl.ANY),
    )(gate, skip, regroup(conv, orders[1]))


def on_device(gate, keys, values, taps, skip_gain):
    devices = lax.axis_size("outer") * lax.axis_size("inner")
    chans, seg = keys.shape
    if chans % devices == 0 and seg % LANES == 0 and devices % 8 == 0:
        return by_channels(gate, keys, values, taps, skip_gain)
    return by_sections(gate, keys, values, taps, skip_gain)


def solution(mesh):
    placed = (
        P(None, ("outer", "inner")),
        P(None, ("outer", "inner")),
        P(None, ("outer", "inner")),
        P(None, ("outer", "inner")),
        P(),
    )
    return jax.shard_map(
        on_device,
        mesh=mesh,
        in_specs=placed,
        out_specs=P(None, ("outer", "inner")),
        check_vma=False,
    )
```

profile of v0, /device:TPU:1, one launch (start us, length us, event | category | flops | bytes accessed | tf_op | source)
XLA Modules:
  0.0 38.5 jit_solution(2578561017145150579)
XLA Ops:
  0.0 0.0 copy-start
  0.0 1.2 %broadcast_multiply_fusion = (f32[128,512]{1,0:T(8,128)S(1)}, f32[128,512]{1,0:T(8,128)S(1)}) fusion(f32[128]{0:T(128)} %param.14, f32[128,512]{1,0:T(8,128)} %param.11, f32[128,512]{1,0:T(8,128)} %param.12), kind=kLoop, calls=%fused_computation | loop fusion | flops 131072 | bytes 1049088 | tf_op jit(solution)/shard_map/mul | solution.py:318
  1.2 0.0 copy-done
  1.2 0.0 copy-start.4
  1.2 0.0 copy-start.5
  1.2 0.1 shard_map.100
  1.3 0.0 copy-start.2
  1.3 0.0 copy-start.3
  1.3 0.0 copy-start.6
  1.3 22.1 %all_to_all.22 = f32[32,32,128]{2,1,0:T(8,128)S(1)} all-to-all(f32[32,32,128]{2,1,0:T(8,128)S(1)} %bitcast.4), channel_id=1, replica_groups={{0,1,2,3,16,17,18,19,20,21,22,23,28,29,30,31,24,25,26,27,8,9,10,11,12,1..., dimensions={0} | all-to-all | bytes 1048576 | tf_op jit(solution)/shard_map/all_to_all | solution.py:315
  23.4 0.0 copy-done.4
  23.4 0.0 copy-done.5
  23.4 0.0 copy-done.2
  23.4 0.0 copy-done.3
  23.4 0.0 copy-done.6
  23.4 1.6 %shard_map.101 = f32[512,128]{1,0:T(8,128)S(1)} custom-call(f32[1024,128]{1,0:T(8,128)S(1)} %bitcast.6, bf16[256,512]{1,0:T(8,128)(2,1)S(1)} %copy-done.4, bf16[1024,256]{1,0:T(8,128)(2,1)S(1)} %copy-done.2, bf16[768,256]{1,0:T(8,128)(2,1)S(1)} %copy-done.3, bf16[128,768]{1,0:T(8,128)(2,1)S(1)} %copy-done.5, f32[2,128,128]{2,1,0:T(8,128)S(1)} %copy-done.6), custom_call_target="tpu_custom_call" | custom-call | flops 1000000000 | bytes 2000000 | tf_op jit(solution)/shard_map/pallas_call | solution.py:321
  25.0 0.0 copy-start.1
  25.0 12.7 %all_to_all.23 = f32[32,16,128]{2,1,0:T(8,128)S(1)} all-to-all(f32[32,16,128]{2,1,0:T(8,128)S(1)} %bitcast.7), channel_id=1, replica_groups={{2,1,3,0,6,5,7,4,10,9,11,8,14,13,15,12,18,17,19,16,22,21,23,20,26,25,27..., dimensions={0} | all-to-all | bytes 524288 | tf_op jit(solution)/shard_map/all_to_all | solution.py:315
  37.8 0.0 copy-done.1
  37.8 0.7 %shard_map.102 = f32[128,512]{1,0:T(8,128)} custom-call(f32[128,512]{1,0:T(8,128)S(1)} %copy-done.1, f32[128,512]{1,0:T(8,128)S(1)} %get-tuple-element.7.skip_ref, f32[512,128]{1,0:T(8,128)S(1)} %bitcast.5), custom_call_target="tpu_custom_call" | custom-call | flops 1000000 | bytes 1048576 | tf_op jit(solution)/shard_map/pallas_call | solution.py:329
Async XLA Ops:
  0.0 1.2 %copy-start = (f32[128,512]{1,0:T(8,128)S(1)}, f32[128,512]{1,0:T(8,128)}, u32[]{:S(2)}) copy-start(f32[128,512]{1,0:T(8,128)} %taps_ref.1) | copy-start | bytes 786436
  1.2 22.2 %copy-start.4 = (bf16[256,512]{1,0:T(8,128)(2,1)S(1)}, bf16[256,512]{1,0:T(8,128)(2,1)}, u32[]{:S(2)}) copy-start(bf16[256,512]{1,0:T(8,128)(2,1)} %constant.10.clone.first_ref) | copy-start | bytes 786436
  1.2 22.2 %copy-start.5 = (bf16[128,768]{1,0:T(8,128)(2,1)S(1)}, bf16[128,768]{1,0:T(8,128)(2,1)}, u32[]{:S(2)}) copy-start(bf16[128,768]{1,0:T(8,128)(2,1)} %constant.13.clone.last_ref) | copy-start | bytes 589828
  1.3 22.1 %copy-start.2 = (bf16[1024,256]{1,0:T(8,128)(2,1)S(1)}, bf16[1024,256]{1,0:T(8,128)(2,1)}, u32[]{:S(2)}) copy-start(bf16[1024,256]{1,0:T(8,128)(2,1)} %constant.11.clone.rows_ref) | copy-start | bytes 1572868
  1.3 22.1 %copy-start.3 = (bf16[768,256]{1,0:T(8,128)(2,1)S(1)}, bf16[768,256]{1,0:T(8,128)(2,1)}, u32[]{:S(2)}) copy-start(bf16[768,256]{1,0:T(8,128)(2,1)} %constant.12.clone.back_ref) | copy-start | bytes 1179652
  1.3 22.1 %copy-start.6 = (f32[2,128,128]{2,1,0:T(8,128)S(1)}, f32[2,128,128]{2,1,0:T(8,128)}, u32[]{:S(2)}) copy-start(f32[2,128,128]{2,1,0:T(8,128)} %constant.14.clone.twiddle_ref) | copy-start | bytes 393220
  25.0 12.7 %copy-start.1 = (f32[128,512]{1,0:T(8,128)S(1)}, f32[128,512]{1,0:T(8,128)}, u32[]{:S(2)}) copy-start(f32[128,512]{1,0:T(8,128)} %gate_ref.1) | copy-start | bytes 786436
where the time goes:
time: 38.7 us; the launch traced here: 38.5 us
  blocking collectives  34.8 us (90%)
  Pallas kernels  2.4 us (6%)
  other arithmetic  1.17 us (3%)
    all_to_all x2, blocking collectives, regroup(): lax.all_to_all(rows, AXES, split_axis=0, concat_axis=0, tiled=True, axis_...  34.8 us
    pallas_call x1, Pallas kernels, by_channels(): on_core(partial(convolve_kernel, devices, own, seg), (chans * tiles, LANE...  1.59 us
    mul x1, other arithmetic, by_channels(): skip_gain[:, None] * product  1.17 us

commit v1 on v0

--- a/solution.py
+++ b/solution.py
@@ -170,8 +170,8 @@
     last_high, last_low = halves(last)
     return (
         np.concatenate([first_high, first_high, first_low, first_low], axis=1),
-        np.concatenate([rows_high, rows_high, rows_high, rows_low], axis=0),
-        np.concatenate([back_high, back_high, back_low], axis=0),
+        np.concatenate([rows_high, rows_low], axis=0),
+        np.concatenate([back_high, back_low], axis=0),
         np.concatenate([last_high, last_high, last_low], axis=1),
         twiddle,
     )
@@ -221,6 +221,15 @@
                     to = first[device] * parts
                     signal_ref[group, to : to + parts, lanes(kind * each + chan)] = data_ref[came : came + parts, :]
 
+    def times(pieces, table_ref):
+        size = table_ref.shape[0] // 2
+        by_high = dot(jnp.concatenate(pieces, axis=0), table_ref[:size, :])
+        total = dot(pieces[0], table_ref[size:, :])
+        rows = total.shape[0]
+        for piece in reversed(range(len(pieces))):
+            total = total + by_high[piece * rows : (piece + 1) * rows]
+        return total
+
     def start(group):
         high, low = split(signal_ref[group])
         return dot(first_ref[...], jnp.concatenate([high, low, high, low], axis=0))
@@ -230,8 +239,7 @@
         for signal in range(2 * each):
             real, imag = begun[:count, lanes(signal)], begun[count:, lanes(signal)]
             turned.append(jnp.concatenate([real * cosine + imag * sine, imag * cosine - real * sine], axis=1))
-        high, low, rest = split(jnp.concatenate(turned, axis=0), 3)
-        return dot(jnp.concatenate([high, low, rest, high], axis=1), rows_ref[...])
+        return times(split(jnp.concatenate(turned, axis=0), 3), rows_ref)
 
     def back(spectrum):
         mid = each * count
@@ -239,8 +247,7 @@
         filt_real, filt_imag = spectrum[mid:, :LANES], spectrum[mid:, LANES:]
         real = sig_real * filt_real - sig_imag * filt_imag
         imag = sig_real * filt_imag + sig_imag * filt_real
-        high, low = split(jnp.concatenate([real, imag], axis=1))
-        return dot(jnp.concatenate([high, low, high], axis=1), back_ref[...])
+        return times(split(jnp.concatenate([real, imag], axis=1)), back_ref)
 
     def end(backed):
         turned = []

time: 38.7 us -> 38.7 us (level)
  no operation moved by 1% of the time
where the time goes in v1:
time: 38.7 us; the launch traced here: 38.5 us
  blocking collectives  34.8 us (90%)
  Pallas kernels  2.4 us (6%)
  other arithmetic  1.17 us (3%)
    all_to_all x2, blocking collectives, regroup(): lax.all_to_all(rows, AXES, split_axis=0, concat_axis=0, tiled=True, axis_...  34.8 us
    pallas_call x1, Pallas kernels, by_channels(): on_core(partial(convolve_kernel, devices, own, seg), (chans * tiles, LANE...  1.59 us
    mul x1, other arithmetic, by_channels(): skip_gain[:, None] * product  1.17 us

profile of v1, /device:TPU:1, one launch (start us, length us, event | category | flops | bytes accessed | tf_op | source)
XLA Modules:
  0.0 38.5 jit_solution(8327982831415183966)
XLA Ops:
  0.0 0.0 copy-start
  0.0 1.2 %broadcast_multiply_fusion = (f32[128,512]{1,0:T(8,128)S(1)}, f32[128,512]{1,0:T(8,128)S(1)}) fusion(f32[128]{0:T(128)} %param.14, f32[128,512]{1,0:T(8,128)} %param.11, f32[128,512]{1,0:T(8,128)} %param.12), kind=kLoop, calls=%fused_computation | loop fusion | flops 131072 | bytes 1049088 | tf_op jit(solution)/shard_map/mul | solution.py:325
  1.2 0.0 copy-done
  1.2 0.0 copy-start.6
  1.2 0.1 shard_map.100
  1.3 0.0 copy-start.2
  1.3 0.0 copy-start.3
  1.3 0.0 copy-start.4
  1.3 0.0 copy-start.5
  1.3 22.1 %all_to_all.22 = f32[32,32,128]{2,1,0:T(8,128)S(1)} all-to-all(f32[32,32,128]{2,1,0:T(8,128)S(1)} %bitcast.4), channel_id=1, replica_groups={{0,1,2,3,16,17,18,19,20,21,22,23,28,29,30,31,24,25,26,27,8,9,10,11,12,1..., dimensions={0} | all-to-all | bytes 1048576 | tf_op jit(solution)/shard_map/all_to_all | solution.py:322
  23.4 0.0 copy-done.6
  23.4 0.0 copy-done.2
  23.4 0.0 copy-done.3
  23.4 0.0 copy-done.4
  23.4 0.0 copy-done.5
  23.4 1.6 %shard_map.101 = f32[512,128]{1,0:T(8,128)S(1)} custom-call(f32[1024,128]{1,0:T(8,128)S(1)} %bitcast.6, bf16[256,512]{1,0:T(8,128)(2,1)S(1)} %copy-done.4, bf16[512,256]{1,0:T(8,128)(2,1)S(1)} %copy-done.3, bf16[512,256]{1,0:T(8,128)(2,1)S(1)} %copy-done.2, bf16[128,768]{1,0:T(8,128)(2,1)S(1)} %copy-done.5, f32[2,128,128]{2,1,0:T(8,128)S(1)} %copy-done.6), custom_call_target="tpu_custom_call" | custom-call | flops 1000000000 | bytes 2000000 | tf_op jit(solution)/shard_map/pallas_call | solution.py:328
  25.0 0.0 copy-start.1
  25.0 12.7 %all_to_all.23 = f32[32,16,128]{2,1,0:T(8,128)S(1)} all-to-all(f32[32,16,128]{2,1,0:T(8,128)S(1)} %bitcast.7), channel_id=1, replica_groups={{2,1,3,0,6,5,7,4,10,9,11,8,14,13,15,12,18,17,19,16,22,21,23,20,26,25,27..., dimensions={0} | all-to-all | bytes 524288 | tf_op jit(solution)/shard_map/all_to_all | solution.py:322
  37.8 0.0 copy-done.1
  37.8 0.7 %shard_map.102 = f32[128,512]{1,0:T(8,128)} custom-call(f32[128,512]{1,0:T(8,128)S(1)} %copy-done.1, f32[128,512]{1,0:T(8,128)S(1)} %get-tuple-element.7.skip_ref, f32[512,128]{1,0:T(8,128)S(1)} %bitcast.5), custom_call_target="tpu_custom_call" | custom-call | flops 1000000 | bytes 1048576 | tf_op jit(solution)/shard_map/pallas_call | solution.py:336
Async XLA Ops:
  0.0 1.2 %copy-start = (f32[128,512]{1,0:T(8,128)S(1)}, f32[128,512]{1,0:T(8,128)}, u32[]{:S(2)}) copy-start(f32[128,512]{1,0:T(8,128)} %taps_ref.1) | copy-start | bytes 786436
  1.2 22.2 %copy-start.6 = (f32[2,128,128]{2,1,0:T(8,128)S(1)}, f32[2,128,128]{2,1,0:T(8,128)}, u32[]{:S(2)}) copy-start(f32[2,128,128]{2,1,0:T(8,128)} %constant.14.clone.twiddle_ref) | copy-start | bytes 393220
  1.3 22.1 %copy-start.2 = (bf16[512,256]{1,0:T(8,128)(2,1)S(1)}, bf16[512,256]{1,0:T(8,128)(2,1)}, u32[]{:S(2)}) copy-start(bf16[512,256]{1,0:T(8,128)(2,1)} %constant.12.clone.back_ref) | copy-start | bytes 786436
  1.3 22.1 %copy-start.3 = (bf16[512,256]{1,0:T(8,128)(2,1)S(1)}, bf16[512,256]{1,0:T(8,128)(2,1)}, u32[]{:S(2)}) copy-start(bf16[512,256]{1,0:T(8,128)(2,1)} %constant.11.clone.rows_ref) | copy-start | bytes 786436
  1.3 22.1 %copy-start.4 = (bf16[256,512]{1,0:T(8,128)(2,1)S(1)}, bf16[256,512]{1,0:T(8,128)(2,1)}, u32[]{:S(2)}) copy-start(bf16[256,512]{1,0:T(8,128)(2,1)} %constant.10.clone.first_ref) | copy-start | bytes 786436
  1.3 22.1 %copy-start.5 = (bf16[128,768]{1,0:T(8,128)(2,1)S(1)}, bf16[128,768]{1,0:T(8,128)(2,1)}, u32[]{:S(2)}) copy-start(bf16[128,768]{1,0:T(8,128)(2,1)} %constant.13.clone.last_ref) | copy-start | bytes 589828
  25.0 12.7 %copy-start.1 = (f32[128,512]{1,0:T(8,128)S(1)}, f32[128,512]{1,0:T(8,128)}, u32[]{:S(2)}) copy-start(f32[128,512]{1,0:T(8,128)} %gate_ref.1) | copy-start | bytes 786436
